TPU v7x, 256 devices: a whole 4x4x8 slice. The times are simulated.
256 devices in a mesh: dom: 64 (over x, z, core), feat: 4 (over y).
Axes of the slice: x: 4, y: 4, z: 8, core: 2. Of those that a mesh axis runs over, the one named last changes fastest.
Arguments:
- node_feats: bfloat16 [128, 851968], P('feat', 'dom'), may hold values from -6 to 6
- adj_cols: int32 [6656, 2], P('dom'), may hold values from 0 to 231, as said below
- adj_vals: bfloat16 [6656, 2, 128, 128], P('dom'), may hold values from -0.375 to 0.375
- send_list: int32 [4096, 2], replicated, may hold values from 0 to 3, as said below
- send_count: int32 [4096], replicated, may hold values from 0 to 2, as said below
- w_self: bfloat16 [128, 256], replicated, may hold values from -0.5 to 0.5
- w_neigh: bfloat16 [128, 256], replicated, may hold values from -0.5 to 0.5
- cotangent: bfloat16 [851968, 256], P(('dom', 'feat')), may hold values from -6 to 6
Outputs:
- out_rows: bfloat16 [851968, 256], P(('dom', 'feat'))
- grad_self: float32 [128, 256], replicated
- grad_neigh: float32 [128, 256], replicated
- grad_feats: bfloat16 [128, 851968], P('feat', 'dom')
Inputs may be any that keep to these rules, and one draw needn't show every extreme that they name: `adj_cols`: entry 0 of a row block names one of the partition's own 13312 / 128 blocks; entries 1 to 1 name halo slots, from 104 on. `send_list`: only the partition's first 4 blocks are ever sent. `send_count`: A partition sends nothing to itself.
All inputs are finite; a program needn't handle non-finite values.
Results may differ from a plain program's by a relative error of at most 0.0058.
Values may be sent and summed in bfloat16 or wider, within the bound.
A program may use at most 128 MiB of HBM per device.

v0:
```python
import math

import jax
import jax.numpy as jnp
from jax import lax
from jax.sharding import PartitionSpec as P


def shards(node_feats, adj_cols, adj_vals, send_list, send_count, w_self, w_neigh, cotangent):
    feat_local, row_count = node_feats.shape
    block_len = adj_vals.shape[-1]
    row_blocks = row_count // block_len
    peer_count = lax.axis_size("dom")
    slot_count = send_list.shape[1]
    own_index = lax.axis_index("dom")
    local_blocks = node_feats.reshape(feat_local, row_blocks, block_len).transpose(1, 0, 2)
    peer_lists = send_list.reshape(peer_count, peer_count, slot_count)
    peer_counts = send_count.reshape(peer_count, peer_count)
    slot_ids = jnp.arange(slot_count, dtype=jnp.int32)
    lists_out = peer_lists[own_index]
    live_out = slot_ids[None, :] < peer_counts[own_index][:, None]
    outgoing = jnp.where(live_out[:, :, None, None], local_blocks[lists_out], 0)
    halo_blocks = lax.all_to_all(outgoing, "dom", split_axis=0, concat_axis=0, tiled=True)
    extended = jnp.concatenate(
        [local_blocks, halo_blocks.reshape(peer_count * slot_count, feat_local, block_len)], axis=0
    )
    picked = extended[adj_cols]
    agg_blocks = jnp.einsum(
        "rkfs,rkts->rft", picked, adj_vals, preferred_element_type=jnp.float32
    ).astype(jnp.bfloat16)
    agg_t = agg_blocks.transpose(1, 0, 2).reshape(feat_local, row_count)
    panels = lax.all_to_all(
        jnp.stack([node_feats, agg_t]), "feat", split_axis=2, concat_axis=1, tiled=True
    )
    weights = jnp.stack([w_self, w_neigh])
    pre = jnp.einsum("gfr,gfh->rh", panels, weights, preferred_element_type=jnp.float32)
    sigmoid_pre = jax.nn.sigmoid(pre)
    out_rows = (pre * sigmoid_pre).astype(jnp.bfloat16)
    grad_pre = (
        cotangent.astype(jnp.float32) * sigmoid_pre * (1.0 + pre * (1.0 - sigmoid_pre))
    ).astype(jnp.bfloat16)
    norm_factor = 1.0 / math.sqrt(row_count * peer_count)
    local_grads_w = jnp.einsum("gfr,rh->gfh", panels, grad_pre, preferred_element_type=jnp.float32)
    weight_sums = lax.psum(local_grads_w, ("dom", "feat")) * norm_factor
    back_panels = jnp.einsum(
        "gfh,rh->gfr", weights, grad_pre, preferred_element_type=jnp.float32
    ).astype(jnp.bfloat16)
    back_panels = lax.all_to_all(back_panels, "feat", split_axis=1, concat_axis=2, tiled=True)
    agg_grad_blocks = back_panels[1].reshape(feat_local, row_blocks, block_len).transpose(1, 0, 2)
    terms = jnp.einsum(
        "rft,rkts->rkfs", agg_grad_blocks, adj_vals, preferred_element_type=jnp.float32
    )
    slot_grads = jax.ops.segment_sum(
        terms.reshape(-1, feat_local, block_len),
        adj_cols.reshape(-1),
        num_segments=row_blocks + peer_count * slot_count,
    )
    local_grads = slot_grads[:row_blocks]
    halo_grads = slot_grads[row_blocks:].reshape(peer_count, slot_count, feat_local, block_len)
    returned = lax.all_to_all(halo_grads, "dom", split_axis=0, concat_axis=0, tiled=True)
    returned = jnp.where(live_out[:, :, None, None], returned, 0.0)
    local_grads = local_grads + jax.ops.segment_sum(
        returned.reshape(-1, feat_local, block_len), lists_out.reshape(-1), num_segments=row_blocks
    )
    grad_feats = back_panels[0].astype(jnp.float32) + local_grads.transpose(1, 0, 2).reshape(
        feat_local, row_count
    )
    return (out_rows, weight_sums[0], weight_sums[1], grad_feats.astype(jnp.bfloat16))


def solution(mesh):
    return jax.shard_map(
        shards,
        mesh=mesh,
        in_specs=(
            P("feat", "dom"),
            P("dom", None),
            P("dom", None, None, None),
            P(),
            P(),
            P(),
            P(),
            P(("dom", "feat"), None),
        ),
        out_specs=(P(("dom", "feat"), None), P(), P(), P("feat", "dom")),
        check_vma=False,
    )
```

profile of v0, /device:TPU:1, one launch (start us, length us, event | category | flops | bytes accessed | tf_op | source)
XLA Modules:
  0.0 501.2 jit_solution(16264842268033248567)
XLA Ops:
  7.2 0.8 reshape.91
  8.0 0.1 iota_compare_fusion
  8.1 1.3 bitcast_bitcast_fusion
  9.4 0.6 copy.71
  10.0 0.1 copy.55
  10.1 0.1 copy.56
  10.2 0.1 reshape.101
  10.4 0.8 gather_fusion
  11.2 0.0 copy-start.10
  11.2 1.2 broadcast_select_fusion.1
  12.3 13.0 %all-to-all-start = ((bf16[64,2,32,128]{3,2,1,0:T(8,128)(2,1)}), bf16[64,2,32,128]{3,2,1,0:T(8,128)(2,1)S(1)}, u32[]{:S(2)}, u32[]{:S(2)}) async-start(bf16[64,2,32,128]{3,2,1,0:T(8,128)(2,1)} %broadcast_select_fusion.1), calls=%async_computation | async-start | bytes 2097152 | tf_op jit(solution)/shard_map/all_to_all | solution.py:23
  25.4 0.1 copy.57
  25.5 0.1 reshape.109
  25.6 28.3 %all-to-all-done = bf16[64,2,32,128]{3,2,1,0:T(8,128)(2,1)S(1)} async-done(((bf16[64,2,32,128]{3,2,1,0:T(8,128)(2,1)}), bf16[64,2,32,128]{3,2,1,0:T(8,128)(2,1)S(1)}, u32[]{:S(2)}, u32[]{:S(2)}) %all-to-all-start) | async-done | bytes 1048608 | tf_op jit(solution)/shard_map/all_to_all | solution.py:23
  53.9 1.0 copy-done.5
  54.9 1.4 pad_maximum_fusion
  56.3 2.0 gather_fusion.1
  58.3 5.9 %fusion.4 = bf16[32,104,128]{2,0,1:T(8,128)(2,1)S(1)} fusion(bf16[104,2,32,128]{3,2,1,0:T(8,128)(2,1)} %bitcast.79, bf16[104,2,128,128]{3,2,1,0:T(8,128)(2,1)} %param.10), kind=kOutput, calls=%fused_computation.18 | convolution fusion | flops 218529792 | bytes 9371648 | tf_op jit(solution)/shard_map/rkfs,rkts->rft/dot_general | solution.py:28
  64.2 0.0 copy-start.6
  64.2 0.3 copy.58
  64.5 0.4 stack_reshape.3
  64.9 0.4 copy-done.6
  65.4 0.2 pad_maximum_fusion.1
  65.5 10.7 %copy.59 = bf16[2,32,13312]{1,0,2:T(2,128)(2,1)} copy(bf16[2,32,13312]{2,1,0:T(8,128)(2,1)S(1)} %pad_maximum_fusion.1) | data formatting | bytes 3407872 | tf_op jit(solution)/shard_map/stack | solution.py:33
  76.2 8.1 %reshape.140 = bf16[4,2,106496]{2,1,0:T(2,128)(2,1)S(1)} reshape(bf16[13312,2,32]{2,1,0:T(2,128)(2,1)} %bitcast.75) | data formatting | bytes 3407872
  84.3 25.9 %all_to_all.43 = bf16[4,2,106496]{2,1,0:T(2,128)(2,1)S(1)} all-to-all(bf16[4,2,106496]{2,1,0:T(2,128)(2,1)S(1)} %reshape.140), channel_id=1, replica_groups=mesh['dom'=64,'feat'=4] {'feat'}, dimensions={0} | all-to-all | bytes 3407872 | tf_op jit(solution)/shard_map/all_to_all | solution.py:32
  110.2 4.9 reshape.141
  115.0 15.7 %copy.72 = bf16[2,32,4,3328]{3,2,1,0:T(4,128)(2,1)S(1)} copy(bf16[2,32,4,3328]{1,0,3,2:T(2,128)(2,1)} %bitcast.76) | data formatting | bytes 3407872 | tf_op jit(solution)/shard_map/all_to_all | solution.py:32
  130.8 0.0 copy-start.7
  130.8 0.0 copy-start.8
  130.8 0.0 copy-start.11
  130.8 0.2 copy.61
  131.0 0.6 copy-done.7
  131.6 0.0 copy-done.8
  131.7 1.3 copy-done.11
  132.9 3.2 multiply_convert_fusion
  136.1 1.3 copy-done
  137.4 0.6 convolution_convert_fusion
  138.0 2.9 copy.63
  141.0 3.6 all-to-all-start.2
  144.5 0.1 copy.65
  144.7 0.1 reshape.117
  144.8 20.7 %all-to-all-done.2 = bf16[2,128,3328]{2,0,1:T(2,128)(2,1)S(1)} async-done(((bf16[2,128,3328]{2,0,1:T(2,128)(2,1)}), bf16[2,128,3328]{2,0,1:T(2,128)(2,1)S(1)}, u32[]{:S(2)}, u32[]{:S(2)}) %all-to-all-start.2) | async-done | bytes 1703968 | tf_op jit(solution)/shard_map/all_to_all | solution.py:48
  165.5 1.3 copy.83
  166.8 1.6 fusion.10
  168.4 1.2 reshape_squeeze.3
  169.6 4.2 fusion.5
  173.8 2.3 broadcast_in_dim.36
  176.1 24.9 %scatter_fusion = f32[232,32,128]{2,1,0:T(8,128)} fusion(f32[232,32,128]{2,1,0:T(8,128)} %broadcast_in_dim.36, s32[208]{0:T(256)S(1)} %reshape.117, f32[208,32,128]{2,1,0:T(8,128)S(1)} %bitcast.77), kind=kCustom, calls=%fused_computation.2 | custom fusion | flops 851968 | bytes 10224448 | tf_op jit(solution)/shard_map/scatter-add | solution.py:53
  201.0 3.1 slice.35
  204.1 8.7 %all-to-all-start.3 = ((f32[64,2,32,128]{3,2,1,0:T(8,128)}), f32[64,2,32,128]{3,2,1,0:T(8,128)}, u32[]{:S(2)}, u32[]{:S(2)}) async-start(f32[64,2,32,128]{3,2,1,0:T(8,128)} %bitcast.27), calls=%async_computation.3 | async-start | bytes 4194304 | tf_op jit(solution)/shard_map/all_to_all | solution.py:60
  212.8 0.0 all-reduce.2.cloned.1.call-start
  212.8 1.3 fusion.2
  214.1 0.0 all-reduce.2.cloned.1.call-update
  214.2 0.1 reshape.125
  214.3 260.0 %all-reduce.2.cloned.1.call-done = f32[2,128,256]{2,1,0:T(8,128)} async-done(((f32[2,128,256]{2,1,0:T(8,128)}), f32[2,128,256]{2,1,0:T(8,128)}) %all-reduce.2.cloned.1.call-update) | async-done | bytes 262160 | tf_op jit(solution)/shard_map/psum | solution.py:44
  474.3 1.0 broadcast_multiply_fusion
  475.3 0.7 slice_bitcast_fusion
  476.0 1.7 slice.34
  477.7 0.2 copy-done.4
  478.0 0.3 copy.75
  478.3 3.1 broadcast_select_fusion
  481.5 11.9 %scatter_fusion.1 = f32[104,32,128]{2,1,0:T(8,128)S(1)} fusion(f32[104,32,128]{2,1,0:T(8,128)S(1)} %slice.34, s32[128]{0:T(128)S(1)} %reshape.125, f32[128,32,128]{2,1,0:T(8,128)} %bitcast.78), kind=kCustom, calls=%fused_computation.3 | custom fusion | flops 524288 | bytes 6291968 | tf_op jit(solution)/shard_map/scatter-add | solution.py:62
  493.3 1.1 fusion
  (19 shorter events, 0.1 us)
Async XLA Ops:
  7.2 2.2 copy-start.9
  11.2 14.2 %copy-start.10 = (s32[104,2]{0,1:T(2,128)S(1)}, s32[104,2]{0,1:T(2,128)}, u32[]{:S(2)}) copy-start(s32[104,2]{0,1:T(2,128)} %param.9) | copy-start | bytes 2500
  12.3 41.5 %all-to-all-start = ((bf16[64,2,32,128]{3,2,1,0:T(8,128)(2,1)}), bf16[64,2,32,128]{3,2,1,0:T(8,128)(2,1)S(1)}, u32[]{:S(2)}, u32[]{:S(2)}) async-start(bf16[64,2,32,128]{3,2,1,0:T(8,128)(2,1)} %broadcast_select_fusion.1), calls=%async_computation | async-start | bytes 2097152 | tf_op jit(solution)/shard_map/all_to_all | solution.py:23
  53.9 1.0 copy-start.5
  64.2 1.2 copy-start.6
  130.8 0.8 copy-start.7
  130.8 0.9 copy-start.8
  130.8 2.1 copy-start.11
  131.0 5.1 %copy-start.2 = (bf16[2,4,32,3328]{3,2,1,0:T(8,128)(2,1)}, bf16[2,4,32,3328]{3,2,1,0:T(8,128)(2,1)S(1)}, u32[]{:S(2)}) copy-start(bf16[2,4,32,3328]{3,2,1,0:T(8,128)(2,1)S(1)} %copy.61) | copy-start | bytes 5111812
  136.1 1.3 copy-start
  141.0 24.5 %all-to-all-start.2 = ((bf16[2,128,3328]{2,0,1:T(2,128)(2,1)}), bf16[2,128,3328]{2,0,1:T(2,128)(2,1)S(1)}, u32[]{:S(2)}, u32[]{:S(2)}) async-start(bf16[2,128,3328]{2,0,1:T(2,128)(2,1)} %copy.63), calls=%async_computation.2 | async-start | bytes 3407872 | tf_op jit(solution)/shard_map/all_to_all | solution.py:48
  204.1 8.7 %copy-start.1 = (bf16[3328,256]{1,0:T(8,128)(2,1)S(1)}, bf16[3328,256]{1,0:T(8,128)(2,1)}, u32[]{:S(2)}) copy-start(bf16[3328,256]{1,0:T(8,128)(2,1)} %copy-done) | copy-start | bytes 5111812
  204.1 8.7 %copy-start.3 = (bf16[2,4,32,3328]{3,2,1,0:T(8,128)(2,1)S(1)}, bf16[2,4,32,3328]{3,2,1,0:T(8,128)(2,1)}, u32[]{:S(2)}) copy-start(bf16[2,4,32,3328]{3,2,1,0:T(8,128)(2,1)} %copy-done.2) | copy-start | bytes 5111812
  204.1 274.2 %all-to-all-start.3 = ((f32[64,2,32,128]{3,2,1,0:T(8,128)}), f32[64,2,32,128]{3,2,1,0:T(8,128)}, u32[]{:S(2)}, u32[]{:S(2)}) async-start(f32[64,2,32,128]{3,2,1,0:T(8,128)} %bitcast.27), calls=%async_computation.3 | async-start | bytes 4194304 | tf_op jit(solution)/shard_map/all_to_all | solution.py:60
  212.8 261.6 %all-reduce.2.cloned.1.call-start = ((), (), s32[]{:S(2)}) async-start(), calls=%async_computation.4 | async-start | bytes 524288 | tf_op jit(solution)/shard_map/psum | solution.py:44
  476.0 2.0 copy-start.4
Sparse Core Ops, SparseCore 0:
  219.6 254.6 all-reduce.1
where the time goes:
time: 504 us; the launch traced here: 501 us
  waiting for transfers between devices  309 us (61%)
  local copies, waits for them, and re-layouts  65.2 us (13%)
  other arithmetic  46.3 us (9%)
  blocking collectives  25.9 us (5%)
  starting transfers between devices  25.3 us (5%)
  matrix products  15.2 us (3%)
  between operations  14.3 us (3%)
    psum x1, waiting for transfers between devices, shards(): weight_sums = lax.psum(local_grads_w, ('dom', 'feat')) * norm_factor  260 us
    all_to_all x1, waiting for transfers between devices, shards(): lax.all_to_all(outgoing, 'dom', split_axis=0, concat_axis=0, tiled=True)  28.3 us
    all_to_all x1, blocking collectives, shards(): lax.all_to_all(jnp.stack([node_feats, agg_t]), 'feat', split_axis=2, conc...  25.9 us
    scatter-add x1, other arithmetic, shards(): jax.ops.segment_sum(terms.reshape(-1, feat_local, block_len), adj_cols.re...  24.9 us
    all_to_all x1, waiting for transfers between devices, shards(): lax.all_to_all(back_panels, 'feat', split_axis=1, concat_axis=2, tiled=True)  20.7 us
    unnamed x28, local copies, waits for them, and re-layouts  18.3 us
    all_to_all x2, local copies, waits for them, and re-layouts, shards(): lax.all_to_all(jnp.stack([node_feats, agg_t]), 'feat', split_axis=2, conc...  15.9 us
    all_to_all x1, starting transfers between devices, shards(): lax.all_to_all(outgoing, 'dom', split_axis=0, concat_axis=0, tiled=True)  13 us
  transfers between devices with their start and end apart: 4, of which 3 were waited for; matrix products, arithmetic and copies ran while one was open for 1% of the time, Pallas kernels for 0%

commit v1 on v0

v1 whole, which is shorter than its diff:
```python
import functools
import math

import jax
import jax.numpy as jnp
from jax import lax
from jax.experimental import pallas as pl
from jax.experimental.pallas import tpu as pltpu
from jax.sharding import PartitionSpec as P

MESH = pl.DeviceIdType.MESH
F32 = jnp.float32
BF16 = jnp.bfloat16

NX, NZ, NC, NY = 4, 8, 2, 4
N_DOM = NX * NZ * NC
CAP = 2
BND = 4
BLK = 128
FL = 32
F = FL * NY
H = 256
RB = 104
RQ = RB // NY
ROWS = RQ * BLK
HALO = N_DOM * BND
JB = 3
HALO_A = N_DOM * JB
PARTS = ((0, 12), (12, 14))
CHUNK = 2 * BLK


def halo_at(c, x, z, j):
    return jnp.where(j < JB, ((c * NX + x) * NZ + z) * JB + j, HALO_A + (c * NZ + z) * NX + x)


def plan_kernel(cols, lists, counts, key, prev0, prev1, last0, last1):
    own = lax.axis_index("dom")

    def clear0(i, carry):
        last0[i] = RB
        return carry

    def clear1(i, carry):
        last1[i] = RB
        return carry

    lax.fori_loop(0, RB, clear0, 0)
    lax.fori_loop(0, HALO + 1, clear1, 0)

    def step(r, carry):
        c0 = cols[0, r]
        prev0[r] = last0[c0]
        last0[c0] = r
        slot = cols[1, r] - RB
        p = slot // CAP
        c = slot % CAP
        entry = p * N_DOM + own
        live = c < counts[entry]
        k = jnp.where(live, halo_at(p % NC, (p // NC) // NZ, (p // NC) % NZ, lists[c, entry]), HALO)
        key[r] = k
        prev1[r] = last1[k]
        last1[k] = r
        return carry

    lax.fori_loop(0, RB, step, 0)


def remote(src, dst, send_sem, recv_sem, **ids):
    return pltpu.make_async_remote_copy(
        src_ref=src, dst_ref=dst, send_sem=send_sem, recv_sem=recv_sem, device_id=ids, device_id_type=MESH
    )


def nt(a, b):
    return lax.dot_general(a, b, (((1,), (1,)), ((), ())), preferred_element_type=F32)


def layer_kernel(
    norm_factor,
    cols,
    key,
    prev0,
    prev1,
    last0,
    last1,
    x_ref,
    ws_ref,
    wn_ref,
    adj_hbm,
    cot_hbm,
    out_hbm,
    gs_ref,
    gn_ref,
    gf_ref,
    adj,
    cot,
    out,
    hal,
    xp,
    ap,
    part,
    aggt,
    gp,
    bpx,
    bpa,
    dx,
    ga,
    xb,
    terms0,
    terms1,
    hg,
    r_core,
    r_x,
    r_z,
    s_x,
    q_z,
    q_x,
    s_z,
    w_all,
    w_x,
    w_xr,
    w_zr,
    w_yr,
    w_c,
    w_cr,
    w_g,
    w_out,
    loc,
    sx,
    rx,
    sa,
    ra,
    sg,
    rg,
    sd,
    rd,
    sh,
    rh,
    sr,
    rr,
    sw,
    rw,
):
    d = lax.axis_index("dom")
    f = lax.axis_index("feat")
    c = d % NC
    z = (d // NC) % NZ
    x = d // (NC * NZ)
    oc = 1 - c

    def at_x(k):
        return lax.rem(x + k, NX)

    def at_z(k):
        return lax.rem(z + k, NZ)

    def at_y(k):
        return lax.rem(f + k, NY)

    def dom(xx, zz, cc):
        return (xx * NZ + zz) * NC + cc

    def to_x(k):
        return {"dom": dom(at_x(k), z, c)}

    def to_z(k):
        return {"dom": dom(x, at_z(k), c)}

    to_core = {"dom": dom(x, z, oc)}

    def to_y(k):
        return {"feat": at_y(k)}

    xs, zs, ys = range(1, NX), range(1, NZ), range(1, NY)

    load_adj = pltpu.make_async_copy(adj_hbm, adj, loc.at[0])
    load_adj.start()
    load_cot = pltpu.make_async_copy(cot_hbm, cot, loc.at[1])
    load_cot.start()

    barrier = pltpu.get_barrier_semaphore()
    partners = [to_x(k) for k in xs] + [to_z(k) for k in zs] + [to_y(k) for k in ys] + [to_core]
    for ids in partners:
        pl.semaphore_signal(barrier, inc=1, device_id=ids, device_id_type=MESH)

    row = c * NX + x

    def b_at(xx, zz, n):
        return pl.ds(((c * NX + xx) * NZ + zz) * JB, n * JB)

    def a_at(zz):
        return pl.ds(HALO_A + (c * NZ + zz) * NX, NX)

    for j in range(JB):
        hal[(row * NZ + z) * JB + j] = x_ref[:, j * BLK : (j + 1) * BLK]
    hal[HALO_A + (c * NZ + z) * NX + x] = x_ref[:, JB * BLK : BND * BLK]
    hal[HALO] = jnp.zeros((FL, BLK), BF16)
    terms0[RB] = jnp.zeros((FL, BLK), F32)
    terms1[RB] = jnp.zeros((FL, BLK), F32)
    pl.semaphore_wait(barrier, len(partners))

    h1z = []
    for k in zs:
        blk = hal.at[b_at(x, z, 1)]
        cp = remote(blk, blk, sh.at[k - 1], rh.at[k - 1], **to_z(k))
        cp.start()
        h1z.append(cp)
    h1x = []
    for k in xs:
        blk = hal.at[HALO_A + (c * NZ + z) * NX + x]
        cp = remote(blk, blk, sh.at[6 + k], rh.at[6 + k], **to_x(k))
        cp.start()
        h1x.append(cp)

    own_cols = pl.ds(pl.multiple_of(f * ROWS, BLK), ROWS)
    own_feats = pl.ds(pl.multiple_of(f * FL, FL), FL)
    xcp = []
    for k in ys:
        q = at_y(k)
        cp = remote(
            x_ref.at[:, pl.ds(pl.multiple_of(q * ROWS, BLK), ROWS)],
            xp.at[own_feats, :],
            sx.at[k - 1],
            rx.at[k - 1],
            **to_y(k),
        )
        cp.start()
        xcp.append(cp)
    own_x = pltpu.make_async_copy(x_ref.at[:, own_cols], xp.at[own_feats, :], loc.at[2])
    own_x.start()

    core_copies = []

    def pass_to_core(blk):
        i = 20 + len(core_copies)
        cp = remote(blk, blk, sh.at[i], rh.at[i], **to_core)
        cp.start()
        core_copies.append(cp)

    for cp in h1x:
        cp.wait()
    col3 = hal.at[a_at(z)]
    h2z = []
    for k in zs:
        cp = remote(col3, col3, sh.at[9 + k], rh.at[9 + k], **to_z(k))
        cp.start()
        h2z.append(cp)
    for cp in h1z:
        cp.wait()
    row3 = hal.at[b_at(x, 0, NZ)]
    h2x = []
    for k in xs:
        cp = remote(row3, row3, sh.at[16 + k], rh.at[16 + k], **to_x(k))
        cp.start()
        h2x.append(cp)
    pass_to_core(col3)
    pass_to_core(row3)

    def to_blocks(r, carry):
        xb[r] = x_ref[:, pl.ds(pl.multiple_of(r * BLK, BLK), BLK)]
        return carry

    lax.fori_loop(0, RB, to_blocks, 0, unroll=8)
    load_adj.wait()

    def local_part(r, carry):
        part[r] = nt(xb[cols[0, r]], adj[r, 0])
        return carry

    lax.fori_loop(0, RB, local_part, 0, unroll=8)

    for k in xs:
        h2x[k - 1].wait()
        pass_to_core(hal.at[b_at(at_x(NX - k), 0, NZ)])
    for k in zs:
        h2z[k - 1].wait()
        pass_to_core(hal.at[a_at(at_z(NZ - k))])
    for cp in core_copies:
        cp.wait()

    acp = []
    own_agg = []
    for n, (first, count) in enumerate(PARTS):
        width = count * BLK
        for k in (1, 2, 3, 0):
            q = at_y(k)
            base = q * RQ + first

            def halo_part(i, carry, base=base):
                r = base + i
                total = part[r] + nt(hal[key[r]], adj[r, 1])
                aggt[:, pl.ds(pl.multiple_of(r * BLK, BLK), BLK)] = total.astype(BF16)
                return carry

            lax.fori_loop(0, count, halo_part, 0, unroll=count // 2)
            src = aggt.at[:, pl.ds(pl.multiple_of(base * BLK, BLK), width)]
            dst = ap.at[own_feats, pl.ds(first * BLK, width)]
            if k:
                i = n * 3 + k - 1
                cp = remote(src, dst, sa.at[i], ra.at[i], **to_y(k))
                acp.append(cp)
            else:
                cp = pltpu.make_async_copy(src, dst, loc.at[3 + n])
                own_agg.append(cp)
            cp.start()

    load_cot.wait()
    own_x.wait()
    for cp in xcp:
        cp.wait()
    weights = jnp.concatenate([ws_ref[...], wn_ref[...]], axis=0)
    gcp = []
    own_g = []
    out_copies = []
    for n, (first, count) in enumerate(PARTS):
        for cp in acp[n * 3 : n * 3 + 3]:
            cp.wait()
        own_agg[n].wait()

        def products(i, carry, first=first):
            at = pl.ds(pl.multiple_of(first * BLK + i * CHUNK, CHUNK if first % 2 == 0 else BLK), CHUNK)
            panel = jnp.concatenate([xp[:, at], ap[:, at]], axis=0)
            pre = jnp.dot(panel.T, weights, preferred_element_type=F32)
            sig = 1.0 / (1.0 + jnp.exp(-pre))
            out[at, :] = (pre * sig).astype(BF16)
            g = (cot[at, :].astype(F32) * sig * (1.0 + pre * (1.0 - sig))).astype(BF16)
            gp[at, :] = g
            back = nt(weights, g).astype(BF16)
            bpx[:, at] = back[:F]
            bpa[:, at] = back[F:]
            return carry

        lax.fori_loop(0, count * BLK // CHUNK, products, 0)
        width = count * BLK
        here = pl.ds(first * BLK, width)
        there = pl.ds(pl.multiple_of(f * ROWS + first * BLK, BLK), width)
        for k in ys:
            i = n * 3 + k - 1
            cp = remote(
                bpa.at[pl.ds(pl.multiple_of(at_y(k) * FL, FL), FL), here],
                ga.at[:, there],
                sg.at[i],
                rg.at[i],
                **to_y(k),
            )
            cp.start()
            gcp.append(cp)
        cp = pltpu.make_async_copy(bpa.at[own_feats, here], ga.at[:, there], loc.at[5 + n])
        cp.start()
        own_g.append(cp)
        cp = pltpu.make_async_copy(out.at[here, :], out_hbm.at[here, :], loc.at[7 + n])
        cp.start()
        out_copies.append(cp)
    dcp = []
    for k in ys:
        cp = remote(
            bpx.at[pl.ds(pl.multiple_of(at_y(k) * FL, FL), FL), :],
            dx.at[:, own_cols],
            sd.at[k - 1],
            rd.at[k - 1],
            **to_y(k),
        )
        cp.start()
        dcp.append(cp)
    own_d = pltpu.make_async_copy(bpx.at[own_feats, :], dx.at[:, own_cols], loc.at[9])
    own_d.start()

    w_all[0:F, :] = jnp.dot(xp[...], gp[...], preferred_element_type=F32)
    w_all[F:, :] = jnp.dot(ap[...], gp[...], preferred_element_type=F32)
    step_x = 2 * F // NX
    step_z = step_x // NZ
    wcp = []
    for k in xs:
        src = w_all.at[pl.ds(pl.multiple_of(at_x(k) * step_x, step_x), step_x), :]
        cp = remote(src, w_xr.at[k - 1], sw.at[k - 1], rw.at[k - 1], **to_x(k))
        cp.start()
        wcp.append(cp)

    def terms_of(q):
        def body(i, carry):
            r = q * RQ + i
            g = ga[:, pl.ds(pl.multiple_of(r * BLK, BLK), BLK)]
            pair = jnp.concatenate([adj[r, 0], adj[r, 1]], axis=1)
            both = jnp.dot(g, pair, preferred_element_type=F32)
            terms0[r] = both[:, :BLK]
            terms1[r] = both[:, BLK:]
            return carry

        lax.fori_loop(0, RQ, body, 0, unroll=13)

    for cp in own_g:
        cp.wait()
    terms_of(f)

    for cp in wcp:
        cp.wait()
    mine = pl.ds(pl.multiple_of(x * step_x, step_x), step_x)
    w_x[...] = w_all[mine, :] + w_xr[0] + w_xr[1] + w_xr[2]
    wcp = []
    for k in zs:
        src = w_x.at[pl.ds(pl.multiple_of(at_z(k) * step_z, step_z), step_z), :]
        cp = remote(src, w_zr.at[k - 1], sw.at[2 + k], rw.at[2 + k], **to_z(k))
        cp.start()
        wcp.append(cp)

    for k in ys:
        for n in range(len(PARTS)):
            gcp[n * 3 + k - 1].wait()
        terms_of(at_y(NY - k))

    def chain(r, carry):
        terms0[r] = terms0[r] + terms0[prev0[r]]
        terms1[r] = terms1[r] + terms1[prev1[r]]
        return carry

    lax.fori_loop(0, RB, chain, 0, unroll=8)

    half_b = NX * NZ * JB
    half_a = NX * NZ

    def collect(base, n):
        def body(b, carry):
            hg[base + b] = terms1[last1[base + b]].astype(BF16)
            return carry

        lax.fori_loop(0, n, body, 0, unroll=8)

    collect(oc * half_b, half_b)
    core_b = remote(hg.at[pl.ds(oc * half_b, half_b)], r_core.at[pl.ds(0, half_b)], sr.at[0], rr.at[0], **to_core)
    core_b.start()
    collect(HALO_A + oc * half_a, half_a)
    core_a = remote(
        hg.at[pl.ds(HALO_A + oc * half_a, half_a)], r_core.at[pl.ds(half_b, half_a)], sr.at[20], rr.at[20], **to_core
    )
    core_a.start()
    collect(c * half_b, half_b)
    collect(HALO_A + c * half_a, half_a)

    for cp in wcp:
        cp.wait()
    acc = w_x[pl.ds(pl.multiple_of(z * step_z, step_z), step_z), :]
    for k in zs:
        acc = acc + w_zr[k - 1]
    w_yr[f] = acc
    wcp = []
    for k in ys:
        cp = remote(w_yr.at[f], w_yr.at[f], sw.at[9 + k], rw.at[9 + k], **to_y(k))
        cp.start()
        wcp.append(cp)

    def add_core(base, first, n):
        def body(b, carry):
            hg[base + b] = (hg[base + b].astype(F32) + r_core[first + b].astype(F32)).astype(BF16)
            return carry

        lax.fori_loop(0, n, body, 0, unroll=8)

    core_b.wait()
    add_core(c * half_b, 0, half_b)
    c1x = []
    for k in xs:
        cp = remote(hg.at[b_at(at_x(k), 0, NZ)], r_x.at[k - 1], sr.at[k], rr.at[k], **to_x(k))
        cp.start()
        c1x.append(cp)
    core_a.wait()
    add_core(HALO_A + c * half_a, half_b, half_a)
    c1z = []
    for k in zs:
        cp = remote(hg.at[a_at(at_z(k))], r_z.at[k - 1], sr.at[3 + k], rr.at[3 + k], **to_z(k))
        cp.start()
        c1z.append(cp)

    for cp in wcp:
        cp.wait()
    w_c[...] = ((w_yr[0] + w_yr[1]) + w_yr[2]) + w_yr[3]
    w_core = remote(w_c, w_cr, sw.at[13], rw.at[13], **to_core)
    w_core.start()

    for cp in c1z:
        cp.wait()
    acc = hg[a_at(z)].astype(F32)
    for k in zs:
        acc = acc + r_z[k - 1].astype(F32)
    s_z[...] = acc.astype(BF16)
    c2x = []
    for k in xs:
        cp = remote(s_z.at[at_x(k)], q_x.at[k - 1], sr.at[10 + k], rr.at[10 + k], **to_x(k))
        cp.start()
        c2x.append(cp)

    w_core.wait()
    w_g[pl.ds(pl.multiple_of(z * step_z, step_z), step_z), :] = (w_c[...] + w_cr[...]) * norm_factor
    wcp = []
    for k in zs:
        src = w_g.at[pl.ds(pl.multiple_of(z * step_z, step_z), step_z), :]
        cp = remote(src, src, sw.at[13 + k], rw.at[13 + k], **to_z(k))
        cp.start()
        wcp.append(cp)

    for cp in c1x:
        cp.wait()
    for zz in range(NZ):
        acc = hg[b_at(x, zz, 1)].astype(F32)
        for k in xs:
            acc = acc + r_x[k - 1, zz * JB : (zz + 1) * JB].astype(F32)
        s_x[zz] = acc.astype(BF16)
    c2z = []
    for k in zs:
        cp = remote(s_x.at[at_z(k)], q_z.at[k - 1], sr.at[13 + k], rr.at[13 + k], **to_z(k))
        cp.start()
        c2z.append(cp)

    for cp in wcp:
        cp.wait()
    w_out[mine, :] = w_g[...]
    wcp = []
    for k in xs:
        cp = remote(w_g, w_out.at[mine, :], sw.at[20 + k], rw.at[20 + k], **to_x(k))
        cp.start()
        wcp.append(cp)

    own_d.wait()
    for cp in dcp:
        cp.wait()

    def finish(s, carry):
        at = pl.ds(pl.multiple_of(s * BLK, BLK), BLK)
        gf_ref[:, at] = (dx[:, at].astype(F32) + terms0[last0[s]]).astype(BF16)
        return carry

    lax.fori_loop(BND, RB, finish, 0, unroll=10)
    for cp in c2x + c2z:
        cp.wait()
    for j in range(BND):
        at = pl.ds(j * BLK, BLK)
        acc = dx[:, at].astype(F32) + terms0[last0[j]]
        if j < JB:
            acc = acc + s_x[z, j].astype(F32)
            for k in zs:
                acc = acc + q_z[k - 1, j].astype(F32)
        else:
            acc = acc + s_z[x].astype(F32)
            for k in xs:
                acc = acc + q_x[k - 1].astype(F32)
        gf_ref[:, at] = acc.astype(BF16)

    for cp in wcp:
        cp.wait()
    gs_ref[...] = w_out[:F, :]
    gn_ref[...] = w_out[F:, :]
    for cp in out_copies:
        cp.wait()


def shards(node_feats, adj_cols, adj_vals, send_list, send_count, w_self, w_neigh, cotangent):
    cols = adj_cols.T
    smem = pl.BlockSpec(memory_space=pltpu.SMEM)
    vmem = pl.BlockSpec(memory_space=pltpu.VMEM)
    hbm = pl.BlockSpec(memory_space=pl.ANY)
    ints = [jax.ShapeDtypeStruct((n,), jnp.int32) for n in (RB, RB, RB, RB, HALO + 1)]
    plan = pl.pallas_call(
        plan_kernel, out_shape=ints, in_specs=[smem] * 3, out_specs=[smem] * 5, name="plan"
    )(cols, send_list.T, send_count)
    vm = pltpu.VMEM
    dma = pltpu.SemaphoreType.DMA
    step_x = 2 * F // NX
    step_z = step_x // NZ
    scratch = [
        vm((RB, 2, BLK, BLK), BF16),
        vm((ROWS, H), BF16),
        vm((ROWS, H), BF16),
        vm((HALO + 1, FL, BLK), BF16),
        vm((F, ROWS), BF16),
        vm((F, ROWS), BF16),
        vm((RB, FL, BLK), F32),
        vm((FL, RB * BLK), BF16),
        vm((ROWS, H), BF16),
        vm((F, ROWS), BF16),
        vm((F, ROWS), BF16),
        vm((FL, RB * BLK), BF16),
        vm((FL, RB * BLK), BF16),
        vm((RB, FL, BLK), BF16),
        vm((RB + 1, FL, BLK), F32),
        vm((RB + 1, FL, BLK), F32),
        vm((HALO, FL, BLK), BF16),
        vm((NX * NZ * BND, FL, BLK), BF16),
        vm((NX - 1, NZ * JB, FL, BLK), BF16),
        vm((NZ - 1, NX, FL, BLK), BF16),
        vm((NZ, JB, FL, BLK), BF16),
        vm((NZ - 1, JB, FL, BLK), BF16),
        vm((NX - 1, FL, BLK), BF16),
        vm((NX, FL, BLK), BF16),
        vm((2 * F, H), F32),
        vm((step_x, H), F32),
        vm((NX - 1, step_x, H), F32),
        vm((NZ - 1, step_z, H), F32),
        vm((NY, step_z, H), F32),
        vm((step_z, H), F32),
        vm((step_z, H), F32),
        vm((step_x, H), F32),
        vm((2 * F, H), F32),
        dma((10,)),
        dma((3,)),
        dma((3,)),
        dma((6,)),
        dma((6,)),
        dma((6,)),
        dma((6,)),
        dma((3,)),
        dma((3,)),
        dma((32,)),
        dma((32,)),
        dma((21,)),
        dma((21,)),
        dma((24,)),
        dma((24,)),
    ]
    return pl.pallas_call(
        functools.partial(layer_kernel, 1.0 / math.sqrt(RB * BLK * N_DOM)),
        out_shape=(
            jax.ShapeDtypeStruct((ROWS, H), BF16),
            jax.ShapeDtypeStruct((F, H), F32),
            jax.ShapeDtypeStruct((F, H), F32),
            jax.ShapeDtypeStruct((FL, RB * BLK), BF16),
        ),
        in_specs=[smem] * 6 + [vmem] * 3 + [hbm] * 2,
        out_specs=(hbm, vmem, vmem, vmem),
        scratch_shapes=scratch,
        compiler_params=pltpu.CompilerParams(
            collective_id=0, has_side_effects=True, vmem_limit_bytes=56 * 1024 * 1024
        ),
        cost_estimate=pl.CostEstimate(flops=1_800_000_000, bytes_accessed=14_000_000, transcendentals=852_000),
        name="layer",
    )(cols, *plan, node_feats, w_self, w_neigh, adj_vals, cotangent)


def solution(mesh):
    return jax.shard_map(
        shards,
        mesh=mesh,
        in_specs=(
            P("feat", "dom"),
            P("dom", None),
            P("dom", None, None, None),
            P(),
            P(),
            P(),
            P(),
            P(("dom", "feat"), None),
        ),
        out_specs=(P(("dom", "feat"), None), P(), P(), P("feat", "dom")),
        check_vma=False,
    )
```

time: 504 us -> 93.6 us (0.19)
  waiting for transfers between devices: 309 us -> 0 us
  Pallas kernels: 0 us -> 87.6 us
  local copies, waits for them, and re-layouts: 65.2 us -> 5.06 us
  other arithmetic: 46.3 us -> 0 us
  blocking collectives: 25.9 us -> 0 us
  starting transfers between devices: 25.3 us -> 0 us
  matrix products: 15.2 us -> 0 us
  between operations: 14.3 us -> 0.67 us
    psum x1 -> x0, waiting for transfers between devices: 260 us -> none  [shards(): weight_sums = lax.psum(local_grads_w, ('dom', 'feat')) * norm_factor]
    pallas_call x0 -> x2, Pallas kernels: none -> 87.6 us  [the longest x1 79.3 us: shards(): pl.pallas_call(functools.partial(layer_kernel, 1.0 / math.sqrt(RB * BLK *...]
    all_to_all x3 -> x0, waiting for transfers between devices: 49 us -> none  [the longest x1 28.3 us: shards(): lax.all_to_all(outgoing, 'dom', split_axis=0, concat_axis=0, tiled=True)]
    scatter-add x2 -> x0, other arithmetic: 36.7 us -> none  [the longest x1 24.9 us: shards(): jax.ops.segment_sum(terms.reshape(-1, feat_local, block_len), adj_cols.re...]
    all_to_all x1 -> x0, blocking collectives: 25.9 us -> none  [shards(): lax.all_to_all(jnp.stack([node_feats, agg_t]), 'feat', split_axis=2, conc...]
    all_to_all x3 -> x0, starting transfers between devices: 25.2 us -> none  [the longest x1 13 us: shards(): lax.all_to_all(outgoing, 'dom', split_axis=0, concat_axis=0, tiled=True)]
    all_to_all x3 -> x0, local copies, waits for them, and re-layouts: 17.2 us -> none  [the longest x2 15.9 us: shards(): lax.all_to_all(jnp.stack([node_feats, agg_t]), 'feat', split_axis=2, conc...]
    dot_general x5 -> x0, matrix products: 15.2 us -> none  [the longest x1 5.88 us: shards(): jnp.einsum('rkfs,rkts->rft', picked, adj_vals, preferred_element_type=jnp...]
  transfers between devices with their start and end apart: 4 -> 0, of which waited for: 3 -> 0; matrix products, arithmetic and copies ran while one was open for 1% -> 0% of each run, Pallas kernels for 0% -> 0%
where the time goes in v1:
time: 93.6 us; the launch traced here: 93.3 us
  Pallas kernels  87.6 us (94%)
  local copies, waits for them, and re-layouts  5.06 us (5%)
    pallas_call x1, Pallas kernels, shards(): pl.pallas_call(functools.partial(layer_kernel, 1.0 / math.sqrt(RB * BLK *...  79.3 us
    pallas_call x1, Pallas kernels, shards(): pl.pallas_call(plan_kernel, out_shape=ints, in_specs=[smem] * 3, out_spec...  8.25 us
    unnamed x10, local copies, waits for them, and re-layouts  5.06 us

profile of v1, /device:TPU:1, one launch (start us, length us, event | category | flops | bytes accessed | tf_op | source)
XLA Modules:
  0.0 93.3 jit_solution(10405490467103362317)
XLA Ops:
  0.6 8.3 %plan.1 = (s32[104]{0:T(128)}, s32[104]{0:T(128)}, s32[104]{0:T(128)}, s32[104]{0:T(128)}, s32[257]{0:T(512)}) custom-call(s32[2,104]{1,0:T(2,128)} %bitcast.3, s32[2,4096]{1,0:T(2,128)} %bitcast.2, s32[4096]{0:T(1024)} %counts.1), custom_call_target="tpu_custom_call" | custom-call | tf_op jit(solution)/shard_map/plan/pallas_call | solution.py:562
  8.9 79.3 %layer.1 = (bf16[3328,256]{1,0:T(8,128)(2,1)}, f32[128,256]{1,0:T(8,128)}, f32[128,256]{1,0:T(8,128)}, bf16[32,13312]{1,0:T(8,128)(2,1)}) custom-call(s32[2,104]{1,0:T(2,128)} %bitcast.4, s32[104]{0:T(128)} %get-tuple-element.9.key, s32[104]{0:T(128)} %get-tuple-element.10.prev0, s32[104]{0:T(128)} %get-tuple-element.11.prev1, s32[104]{0:T(128)} %get-tuple-element.12.last0, ...), custom_call_target="tpu_custom_call" | custom-call | flops 1800000000 | bytes 14000000 | tf_op jit(solution)/shard_map/layer/pallas_call | solution.py:619
  88.2 0.0 copy-start.2
  88.2 0.0 copy-start.1
  88.3 0.0 copy-start
  88.3 2.8 %copy.16 = bf16[3328,256]{1,0:T(8,128)(2,1)} copy(bf16[3328,256]{1,0:T(8,128)(2,1)} %get-tuple-element.18) | data formatting | bytes 3407872
  91.1 0.0 copy-done.2
  91.1 0.7 copy.17
  91.8 0.0 copy-done.1
  91.8 0.7 copy.18
  92.4 0.0 copy-done
  92.4 0.9 copy.19
Async XLA Ops:
  88.2 2.9 %copy-start.2 = (f32[128,256]{1,0:T(8,128)S(1)}, f32[128,256]{1,0:T(8,128)}, u32[]{:S(2)}) copy-start(f32[128,256]{1,0:T(8,128)} %get-tuple-element.19) | copy-start | bytes 393220
  88.2 3.5 %copy-start.1 = (f32[128,256]{1,0:T(8,128)S(1)}, f32[128,256]{1,0:T(8,128)}, u32[]{:S(2)}) copy-start(f32[128,256]{1,0:T(8,128)} %get-tuple-element.20) | copy-start | bytes 393220
  88.3 4.2 %copy-start = (bf16[32,13312]{1,0:T(8,128)(2,1)S(1)}, bf16[32,13312]{1,0:T(8,128)(2,1)}, u32[]{:S(2)}) copy-start(bf16[32,13312]{1,0:T(8,128)(2,1)} %get-tuple-element.21) | copy-start | bytes 2555908

commit v2 on v1

v2 whole, which is shorter than its diff:
```python
import functools
import math

import jax
import jax.numpy as jnp
from jax import lax
from jax.experimental import pallas as pl
from jax.experimental.pallas import tpu as pltpu
from jax.sharding import PartitionSpec as P

MESH = pl.DeviceIdType.MESH
F32 = jnp.float32
BF16 = jnp.bfloat16

NX, NZ, NC, NY = 4, 8, 2, 4
N_DOM = NX * NZ * NC
CAP = 2
BND = 4
BLK = 128
FL = 32
F = FL * NY
H = 256
RB = 104
RQ = RB // NY
ROWS = RQ * BLK
HALO = N_DOM * BND
JB = 3
HALO_A = N_DOM * JB
PARTS = ((0, 8), (8, 8), (16, 10))
CHUNK = 2 * BLK
OFFSET = (0, 1, 7, 2, 6, 3, 5, 4)
GROUPS = ((0, 1), (1, 2), (3, 2), (5, 3))


def slot_of(delta):
    return jnp.where(delta <= 4, jnp.maximum(2 * delta - 1, 0), 2 * (NZ - delta))


def make_plan(d, z, cols, lists, counts, cols_v, tab):
    lane32 = lax.broadcasted_iota(jnp.int32, (NX * NZ, BLK), 1)
    chip = lax.broadcasted_iota(jnp.int32, (NX * NZ, 1), 0)
    xx, m = chip // NZ, slot_of(lax.rem(chip % NZ - z + NZ, NZ))
    cols_v[...] = jnp.zeros_like(cols_v)
    cols_v[0:2, 0:RB] = cols[...]
    c0 = cols_v[0:1, :]
    entry = cols_v[1:2, :] - RB
    key = jnp.zeros((NX * NZ, BLK), jnp.int32)
    for core in range(NC):
        here = lane32 == core * N_DOM + d
        count = jnp.sum(jnp.where(here, counts[...], 0), axis=1, keepdims=True)
        for slot in range(CAP):
            j = jnp.sum(jnp.where(here, lists[:, slot, :], 0), axis=1, keepdims=True)
            at_b = ((core * NX + xx) * NZ + m) * JB + j
            at_a = HALO_A + (core * NZ + m) * NX + xx
            at = jnp.where(slot < count, jnp.where(j < JB, at_b, at_a), HALO)
            reads = entry == chip * (NC * CAP) + core * CAP + slot
            key = key + jnp.where(reads, at, 0)
    key = jnp.sum(key, axis=0, keepdims=True)
    r = lax.broadcasted_iota(jnp.int32, (BLK, BLK), 0)
    lane = lax.broadcasted_iota(jnp.int32, (BLK, BLK), 1)
    c0_t = jnp.broadcast_to(c0, (BLK, BLK)).T
    key_t = jnp.broadcast_to(key, (BLK, BLK)).T

    def latest(mask):
        top = jnp.max(jnp.where(mask & (r < RB), r, -1), axis=0, keepdims=True)
        return jnp.where(top < 0, RB, top)

    tab[0:1, :] = key
    tab[1:2, :] = latest((c0_t == c0) & (r < lane))
    tab[2:3, :] = latest((key_t == key) & (r < lane))
    tab[3:4, :] = latest(c0_t == lane)
    tab[4:5, :] = latest(key_t == lane)
    tab[5:6, :] = latest(key_t == lane + BLK)
    tab[6:8, :] = jnp.zeros((2, BLK), jnp.int32)


def remote(src, dst, send_sem, recv_sem, **ids):
    return pltpu.make_async_remote_copy(
        src_ref=src, dst_ref=dst, send_sem=send_sem, recv_sem=recv_sem, device_id=ids, device_id_type=MESH
    )


def nt(a, b):
    return lax.dot_general(a, b, (((1,), (1,)), ((), ())), preferred_element_type=F32)


def layer_kernel(
    norm_factor,
    cols,
    cols_ref,
    lists,
    counts,
    ws_ref,
    wn_ref,
    x_hbm,
    adj_hbm,
    cot_hbm,
    out_hbm,
    gs_ref,
    gn_ref,
    gf_ref,
    x_ref,
    adj,
    cot,
    out,
    hal,
    xp,
    ap,
    aggt,
    gp,
    bpx,
    bpa,
    dx,
    ga,
    xb,
    terms0,
    terms1,
    hg,
    r_core,
    r_x,
    r_z,
    s_x,
    q_z,
    q_x,
    s_z,
    w_all,
    w_x,
    w_xr,
    w_zr,
    w_yr,
    w_c,
    w_cr,
    w_g,
    w_out,
    cols_v,
    tab,
    plan,
    loc,
    sx,
    rx,
    sa,
    ra,
    sg,
    rg,
    sd,
    rd,
    sh,
    rh,
    sr,
    rr,
    sw,
    rw,
):
    d = lax.axis_index("dom")
    f = lax.axis_index("feat")
    c = d % NC
    z = (d // NC) % NZ
    x = d // (NC * NZ)
    oc = 1 - c

    def at_x(k):
        return lax.rem(x + k, NX)

    def at_z(k):
        return lax.rem(z + k, NZ)

    def at_y(k):
        return lax.rem(f + k, NY)

    def dom(xx, zz, cc):
        return (xx * NZ + zz) * NC + cc

    def to_x(k):
        return {"dom": dom(at_x(k), z, c)}

    def to_z(k):
        return {"dom": dom(x, at_z(k), c)}

    to_core = {"dom": dom(x, z, oc)}

    def to_y(k):
        return {"feat": at_y(k)}

    xs, zs, ys = range(1, NX), range(1, NZ), range(1, NY)

    barrier = pltpu.get_barrier_semaphore()
    partners = [to_x(k) for k in xs] + [to_z(k) for k in zs] + [to_y(k) for k in ys] + [to_core]
    for ids in partners:
        pl.semaphore_signal(barrier, inc=1, device_id=ids, device_id_type=MESH)

    own_b = (c * NX + x) * NZ * JB
    own_a = HALO_A + c * NZ * NX + x
    load_own = []
    for j in range(BND):
        at = own_b + j if j < JB else own_a
        cp = pltpu.make_async_copy(x_hbm.at[:, pl.ds(j * BLK, BLK)], hal.at[at], loc.at[11 + j])
        cp.start()
        load_own.append(cp)
    load_x = pltpu.make_async_copy(x_hbm, x_ref, loc.at[15])
    load_x.start()
    load_adj = pltpu.make_async_copy(adj_hbm, adj, loc.at[0])
    load_cot = pltpu.make_async_copy(cot_hbm, cot, loc.at[1])

    def b_at(xx, slot, n):
        return pl.ds(((c * NX + xx) * NZ + slot) * JB, n * JB)

    def a_at(slot, n=1):
        return pl.ds(HALO_A + (c * NZ + slot) * NX, n * NX)

    hal[HALO] = jnp.zeros((FL, BLK), BF16)
    terms0[RB] = jnp.zeros((FL, BLK), F32)
    terms1[RB] = jnp.zeros((FL, BLK), F32)
    for cp in load_own:
        cp.wait()
    pl.semaphore_wait(barrier, len(partners))

    def back_slot(m):
        return OFFSET.index((NZ - OFFSET[m]) % NZ)

    h1z = [None]
    for m in range(1, NZ):
        cp = remote(hal.at[b_at(x, 0, 1)], hal.at[b_at(x, back_slot(m), 1)], sh.at[m], rh.at[m], **to_z(OFFSET[m]))
        cp.start()
        h1z.append(cp)
    h1x = []
    for k in xs:
        blk = hal.at[own_a]
        cp = remote(blk, blk, sh.at[7 + k], rh.at[7 + k], **to_x(k))
        cp.start()
        h1x.append(cp)
    h2x = []

    def along_x(g):
        first, n = GROUPS[g]
        blk = hal.at[b_at(x, first, n)]
        row = []
        for k in xs:
            i = 10 + g * 3 + k
            cp = remote(blk, blk, sh.at[i], rh.at[i], **to_x(k))
            cp.start()
            row.append(cp)
        h2x.append(row)

    along_x(0)

    own_cols = pl.ds(pl.multiple_of(f * ROWS, BLK), ROWS)
    own_feats = pl.ds(pl.multiple_of(f * FL, FL), FL)
    load_x.wait()
    load_adj.start()
    xcp = []
    for k in ys:
        q = at_y(k)
        cp = remote(
            x_ref.at[:, pl.ds(pl.multiple_of(q * ROWS, BLK), ROWS)],
            xp.at[own_feats, :],
            sx.at[k - 1],
            rx.at[k - 1],
            **to_y(k),
        )
        cp.start()
        xcp.append(cp)
    own_x = pltpu.make_async_copy(x_ref.at[:, own_cols], xp.at[own_feats, :], loc.at[2])
    own_x.start()
    load_cot.start()

    core_copies = []

    def pass_to_core(at):
        i = 30 + len(core_copies)
        cp = remote(hal.at[at], hal.at[at], sh.at[i], rh.at[i], **to_core)
        cp.start()
        core_copies.append(cp)

    for cp in h1x:
        cp.wait()
    h2z = [None]
    for m in range(1, NZ):
        cp = remote(hal.at[a_at(0)], hal.at[a_at(back_slot(m))], sh.at[22 + m], rh.at[22 + m], **to_z(OFFSET[m]))
        cp.start()
        h2z.append(cp)

    make_plan(d, z, cols_ref, lists, counts, cols_v, tab)
    load_plan = pltpu.make_async_copy(tab, plan, loc.at[10])
    load_plan.start()

    def to_blocks(r, carry):
        xb[r] = x_ref[:, pl.ds(pl.multiple_of(r * BLK, BLK), BLK)]
        return carry

    for m in (1, 2):
        h1z[m].wait()
    along_x(1)
    lax.fori_loop(0, RB, to_blocks, 0, unroll=8)
    for m in (3, 4):
        h1z[m].wait()
    along_x(2)
    for m in (5, 6, 7):
        h1z[m].wait()
    along_x(3)
    pass_to_core(b_at(x, 0, NZ))
    for m in (1, 2):
        h2z[m].wait()
    pass_to_core(a_at(0, 3))
    for k in xs:
        for g in (0, 1, 2):
            h2x[g][k - 1].wait()
    for k in xs:
        pass_to_core(b_at(at_x(NX - k), 0, 5))
    for m in (3, 4):
        h2z[m].wait()
    pass_to_core(a_at(3, 2))
    load_plan.wait()
    for m in (5, 6, 7):
        h2z[m].wait()
    pass_to_core(a_at(5, 3))
    for k in xs:
        h2x[3][k - 1].wait()
        pass_to_core(b_at(at_x(NX - k), 5, 3))
    for cp in core_copies:
        cp.wait()

    load_adj.wait()
    acp = []
    own_agg = []
    for n, (first, count) in enumerate(PARTS):
        width = count * BLK
        for k in (1, 2, 3, 0):
            q = at_y(k)
            base = q * RQ + first

            def aggregate(i, carry, base=base):
                r = base + i
                sources = jnp.concatenate([xb[cols[0, r]], hal[plan[0, r]]], axis=1)
                total = nt(sources, jnp.concatenate([adj[r, 0], adj[r, 1]], axis=1))
                aggt[:, pl.ds(pl.multiple_of(r * BLK, BLK), BLK)] = total.astype(BF16)
                return carry

            lax.fori_loop(0, count, aggregate, 0, unroll=count // 2)
            src = aggt.at[:, pl.ds(pl.multiple_of(base * BLK, BLK), width)]
            dst = ap.at[own_feats, pl.ds(first * BLK, width)]
            if k:
                i = n * 3 + k - 1
                cp = remote(src, dst, sa.at[i], ra.at[i], **to_y(k))
                acp.append(cp)
            else:
                cp = pltpu.make_async_copy(src, dst, loc.at[16 + n])
                own_agg.append(cp)
            cp.start()

    load_cot.wait()
    own_x.wait()
    for cp in xcp:
        cp.wait()
    weights = jnp.concatenate([ws_ref[...], wn_ref[...]], axis=0)
    gcp = []
    own_g = []
    out_copies = []
    for n, (first, count) in enumerate(PARTS):
        for cp in acp[n * 3 : n * 3 + 3]:
            cp.wait()
        own_agg[n].wait()

        def products(i, carry, first=first):
            at = pl.ds(pl.multiple_of(first * BLK + i * CHUNK, CHUNK), CHUNK)
            panel = jnp.concatenate([xp[:, at], ap[:, at]], axis=0)
            pre = jnp.dot(panel.T, weights, preferred_element_type=F32)
            sig = 1.0 / (1.0 + jnp.exp(-pre))
            out[at, :] = (pre * sig).astype(BF16)
            g = (cot[at, :].astype(F32) * sig * (1.0 + pre * (1.0 - sig))).astype(BF16)
            gp[at, :] = g
            back = nt(weights, g).astype(BF16)
            bpx[:, at] = back[:F]
            bpa[:, at] = back[F:]
            return carry

        lax.fori_loop(0, count * BLK // CHUNK, products, 0)
        width = count * BLK
        here = pl.ds(first * BLK, width)
        there = pl.ds(pl.multiple_of(f * ROWS + first * BLK, BLK), width)
        for k in ys:
            i = n * 3 + k - 1
            cp = remote(
                bpa.at[pl.ds(pl.multiple_of(at_y(k) * FL, FL), FL), here],
                ga.at[:, there],
                sg.at[i],
                rg.at[i],
                **to_y(k),
            )
            cp.start()
            gcp.append(cp)
        cp = pltpu.make_async_copy(bpa.at[own_feats, here], ga.at[:, there], loc.at[19 + n])
        cp.start()
        own_g.append(cp)
        cp = pltpu.make_async_copy(out.at[here, :], out_hbm.at[here, :], loc.at[22 + n])
        cp.start()
        out_copies.append(cp)
    dcp = []
    for k in ys:
        cp = remote(
            bpx.at[pl.ds(pl.multiple_of(at_y(k) * FL, FL), FL), :],
            dx.at[:, own_cols],
            sd.at[k - 1],
            rd.at[k - 1],
            **to_y(k),
        )
        cp.start()
        dcp.append(cp)
    own_d = pltpu.make_async_copy(bpx.at[own_feats, :], dx.at[:, own_cols], loc.at[9])
    own_d.start()

    def add_core(base, first, n):
        def body(b, carry):
            hg[base + b] = (hg[base + b].astype(F32) + r_core[first + b].astype(F32)).astype(BF16)
            return carry

        lax.fori_loop(0, n, body, 0, unroll=8)

    w_all[0:F, :] = jnp.dot(xp[...], gp[...], preferred_element_type=F32)
    w_all[F:, :] = jnp.dot(ap[...], gp[...], preferred_element_type=F32)
    step_x = 2 * F // NX
    step_z = step_x // NZ
    wcp = []
    for k in xs:
        src = w_all.at[pl.ds(pl.multiple_of(at_x(k) * step_x, step_x), step_x), :]
        cp = remote(src, w_xr.at[k - 1], sw.at[k - 1], rw.at[k - 1], **to_x(k))
        cp.start()
        wcp.append(cp)

    def terms_of(q, first, count):
        def body(i, carry):
            r = q * RQ + first + i
            g = ga[:, pl.ds(pl.multiple_of(r * BLK, BLK), BLK)]
            pair = jnp.concatenate([adj[r, 0], adj[r, 1]], axis=1)
            both = jnp.dot(g, pair, preferred_element_type=F32)
            terms0[r] = both[:, :BLK]
            terms1[r] = both[:, BLK:]
            return carry

        lax.fori_loop(0, count, body, 0, unroll=count // 2)

    for cp in own_g:
        cp.wait()
    terms_of(f, 0, RQ)

    for cp in wcp:
        cp.wait()
    mine = pl.ds(pl.multiple_of(x * step_x, step_x), step_x)
    w_x[...] = w_all[mine, :] + w_xr[0] + w_xr[1] + w_xr[2]
    wcp = []
    for k in zs:
        src = w_x.at[pl.ds(pl.multiple_of(at_z(k) * step_z, step_z), step_z), :]
        cp = remote(src, w_zr.at[k - 1], sw.at[2 + k], rw.at[2 + k], **to_z(k))
        cp.start()
        wcp.append(cp)

    for n, (first, count) in enumerate(PARTS):
        for k in ys:
            gcp[n * 3 + k - 1].wait()
            terms_of(at_y(NY - k), first, count)

    def chain(r, carry):
        terms0[r] = terms0[r] + terms0[plan[1, r]]
        terms1[r] = terms1[r] + terms1[plan[2, r]]
        return carry

    lax.fori_loop(0, RB, chain, 0, unroll=8)

    half_b = NX * NZ * JB
    half_a = NX * NZ

    def collect(base, n):
        def body(b, carry):
            at = base + b
            hg[at] = terms1[plan[4 + at // BLK, at % BLK]].astype(BF16)
            return carry

        lax.fori_loop(0, n, body, 0, unroll=8)

    row_b = NZ * JB
    core_copies = []
    for i, k in enumerate((1, 3, 2, 0)):
        first = at_x(k) * row_b
        collect(oc * half_b + first, row_b)
        cp = remote(
            hg.at[pl.ds(oc * half_b + first, row_b)], r_core.at[pl.ds(first, row_b)], sr.at[i], rr.at[i], **to_core
        )
        cp.start()
        core_copies.append(cp)
        if i == 2:
            collect(HALO_A + oc * half_a, half_a)
            core_a = remote(
                hg.at[pl.ds(HALO_A + oc * half_a, half_a)],
                r_core.at[pl.ds(half_b, half_a)],
                sr.at[4],
                rr.at[4],
                **to_core,
            )
            core_a.start()
    collect(c * half_b, half_b)
    collect(HALO_A + c * half_a, half_a)

    for cp in wcp:
        cp.wait()
    acc = w_x[pl.ds(pl.multiple_of(z * step_z, step_z), step_z), :]
    for k in zs:
        acc = acc + w_zr[k - 1]
    w_yr[f] = acc
    wcp = []
    for k in ys:
        cp = remote(w_yr.at[f], w_yr.at[f], sw.at[9 + k], rw.at[9 + k], **to_y(k))
        cp.start()
        wcp.append(cp)

    for i, k in enumerate((1, 3, 2)):
        core_copies[i].wait()
        add_core(c * half_b + at_x(k) * row_b, at_x(k) * row_b, row_b)
    c1x = [None] * len(GROUPS)
    for g in (3, 2, 1, 0):
        first, n = GROUPS[g]
        c1x[g] = []
        for k in xs:
            i = 4 + g * 3 + k
            cp = remote(
                hg.at[b_at(at_x(k), first, n)],
                r_x.at[k - 1, pl.ds(first * JB, n * JB)],
                sr.at[i],
                rr.at[i],
                **to_x(k),
            )
            cp.start()
            c1x[g].append(cp)
    core_a.wait()
    add_core(HALO_A + c * half_a, half_b, half_a)
    c1z = []
    for m in range(1, NZ):
        cp = remote(hg.at[a_at(m)], r_z.at[m - 1], sr.at[16 + m], rr.at[16 + m], **to_z(OFFSET[m]))
        cp.start()
        c1z.append(cp)
    for cp in wcp:
        cp.wait()
    w_c[...] = ((w_yr[0] + w_yr[1]) + w_yr[2]) + w_yr[3]
    w_core = remote(w_c, w_cr, sw.at[13], rw.at[13], **to_core)
    w_core.start()

    core_copies[3].wait()
    add_core(c * half_b + x * row_b, x * row_b, row_b)
    w_core.wait()
    w_g[pl.ds(pl.multiple_of(z * step_z, step_z), step_z), :] = (w_c[...] + w_cr[...]) * norm_factor
    wcp = []
    for k in zs:
        src = w_g.at[pl.ds(pl.multiple_of(z * step_z, step_z), step_z), :]
        cp = remote(src, src, sw.at[13 + k], rw.at[13 + k], **to_z(k))
        cp.start()
        wcp.append(cp)

    c2z = []
    for g in (3, 2, 1, 0):
        for cp in c1x[g]:
            cp.wait()
        first, n = GROUPS[g]
        for m in range(first, first + n):
            at = slice(m * JB, (m + 1) * JB)
            acc = hg[b_at(x, m, 1)].astype(F32)
            for k in xs:
                acc = acc + r_x[k - 1, at].astype(F32)
            s_x[m] = acc.astype(BF16)
            if m:
                cp = remote(s_x.at[m], q_z.at[m - 1], sr.at[26 + m], rr.at[26 + m], **to_z(OFFSET[m]))
                cp.start()
                c2z.append(cp)
        if g == 2:
            for cp in c1z:
                cp.wait()
            acc = hg[a_at(0)].astype(F32)
            for k in zs:
                acc = acc + r_z[k - 1].astype(F32)
            s_z[...] = acc.astype(BF16)
            c2x = []
            for k in xs:
                cp = remote(s_z.at[at_x(k)], q_x.at[k - 1], sr.at[23 + k], rr.at[23 + k], **to_x(k))
                cp.start()
                c2x.append(cp)
        if g == 1:
            for cp in wcp:
                cp.wait()
            w_out[mine, :] = w_g[...]
            wcp = []
            for k in xs:
                cp = remote(w_g, w_out.at[mine, :], sw.at[20 + k], rw.at[20 + k], **to_x(k))
                cp.start()
                wcp.append(cp)

    own_d.wait()
    for cp in dcp:
        cp.wait()

    def finish(s, carry):
        at = pl.ds(pl.multiple_of(s * BLK, BLK), BLK)
        gf_ref[:, at] = (dx[:, at].astype(F32) + terms0[plan[3, s]]).astype(BF16)
        return carry

    lax.fori_loop(BND, RB, finish, 0, unroll=10)
    for cp in c2x + c2z:
        cp.wait()
    for j in range(BND):
        at = pl.ds(j * BLK, BLK)
        acc = dx[:, at].astype(F32) + terms0[plan[3, j]]
        if j < JB:
            acc = acc + s_x[0, j].astype(F32)
            for k in zs:
                acc = acc + q_z[k - 1, j].astype(F32)
        else:
            acc = acc + s_z[x].astype(F32)
            for k in xs:
                acc = acc + q_x[k - 1].astype(F32)
        gf_ref[:, at] = acc.astype(BF16)

    for cp in wcp:
        cp.wait()
    gs_ref[...] = w_out[:F, :]
    gn_ref[...] = w_out[F:, :]
    for cp in out_copies:
        cp.wait()


def emit_kernel(*refs):
    copies = [pltpu.make_async_copy(refs[i], refs[4 + i], refs[8].at[i]) for i in range(4)]
    for cp in copies:
        cp.start()
    for cp in copies:
        cp.wait()


def shards(node_feats, adj_cols, adj_vals, send_list, send_count, w_self, w_neigh, cotangent):
    cols = adj_cols.T
    lists = send_list.reshape(NX * NZ, NC * N_DOM, CAP).transpose(0, 2, 1)
    counts = send_count.reshape(NX * NZ, NC * N_DOM)
    smem = pl.BlockSpec(memory_space=pltpu.SMEM)
    vmem = pl.BlockSpec(memory_space=pltpu.VMEM)
    hbm = pl.BlockSpec(memory_space=pl.ANY)
    vm = pltpu.VMEM
    dma = pltpu.SemaphoreType.DMA
    step_x = 2 * F // NX
    step_z = step_x // NZ
    scratch = [
        vm((FL, RB * BLK), BF16),
        vm((RB, 2, BLK, BLK), BF16),
        vm((ROWS, H), BF16),
        vm((ROWS, H), BF16),
        vm((HALO + 1, FL, BLK), BF16),
        vm((F, ROWS), BF16),
        vm((F, ROWS), BF16),
        vm((FL, RB * BLK), BF16),
        vm((ROWS, H), BF16),
        vm((F, ROWS), BF16),
        vm((F, ROWS), BF16),
        vm((FL, RB * BLK), BF16),
        vm((FL, RB * BLK), BF16),
        vm((RB, FL, BLK), BF16),
        vm((RB + 1, FL, BLK), F32),
        vm((RB + 1, FL, BLK), F32),
        vm((HALO, FL, BLK), BF16),
        vm((NX * NZ * BND, FL, BLK), BF16),
        vm((NX - 1, NZ * JB, FL, BLK), BF16),
        vm((NZ - 1, NX, FL, BLK), BF16),
        vm((NZ, JB, FL, BLK), BF16),
        vm((NZ - 1, JB, FL, BLK), BF16),
        vm((NX - 1, FL, BLK), BF16),
        vm((NX, FL, BLK), BF16),
        vm((2 * F, H), F32),
        vm((step_x, H), F32),
        vm((NX - 1, step_x, H), F32),
        vm((NZ - 1, step_z, H), F32),
        vm((NY, step_z, H), F32),
        vm((step_z, H), F32),
        vm((step_z, H), F32),
        vm((step_x, H), F32),
        vm((2 * F, H), F32),
        vm((8, BLK), jnp.int32),
        vm((8, BLK), jnp.int32),
        pltpu.SMEM((8, BLK), jnp.int32),
        dma((25,)),
        dma((3,)),
        dma((3,)),
        dma((9,)),
        dma((9,)),
        dma((9,)),
        dma((9,)),
        dma((3,)),
        dma((3,)),
        dma((42,)),
        dma((42,)),
        dma((34,)),
        dma((34,)),
        dma((24,)),
        dma((24,)),
    ]
    results = pl.pallas_call(
        functools.partial(layer_kernel, 1.0 / math.sqrt(RB * BLK * N_DOM)),
        out_shape=(
            jax.ShapeDtypeStruct((ROWS, H), BF16),
            jax.ShapeDtypeStruct((F, H), F32),
            jax.ShapeDtypeStruct((F, H), F32),
            jax.ShapeDtypeStruct((FL, RB * BLK), BF16),
        ),
        in_specs=[smem] + [vmem] * 5 + [hbm] * 3,
        out_specs=(hbm, vmem, vmem, vmem),
        scratch_shapes=scratch,
        compiler_params=pltpu.CompilerParams(
            collective_id=0, has_side_effects=True, vmem_limit_bytes=56 * 1024 * 1024
        ),
        cost_estimate=pl.CostEstimate(flops=1_800_000_000, bytes_accessed=14_000_000, transcendentals=852_000),
        name="layer",
    )(cols, cols, lists, counts, w_self, w_neigh, node_feats, adj_vals, cotangent)
    return pl.pallas_call(
        emit_kernel,
        out_shape=[jax.ShapeDtypeStruct(a.shape, a.dtype) for a in results],
        in_specs=[vmem] * 4,
        out_specs=[hbm] * 4,
        scratch_shapes=[dma((4,))],
        name="emit",
    )(*results)


def solution(mesh):
    return jax.shard_map(
        shards,
        mesh=mesh,
        in_specs=(
            P("feat", "dom"),
            P("dom", None),
            P("dom", None, None, None),
            P(),
            P(),
            P(),
            P(),
            P(("dom", "feat"), None),
        ),
        out_specs=(P(("dom", "feat"), None), P(), P(), P("feat", "dom")),
        check_vma=False,
    )
```

time: 93.6 us -> 76.4 us (0.82)
  Pallas kernels: 87.6 us -> 74.9 us
  local copies, waits for them, and re-layouts: 5.06 us -> 0 us
    pallas_call x1, Pallas kernels: 79.3 us -> 71.5 us  [shards(): pl.pallas_call(functools.partial(layer_kernel, 1.0 / math.sqrt(RB * BLK *...]
    unnamed x10 -> x0, local copies, waits for them, and re-layouts: 5.06 us -> none
    pallas_call x1, Pallas kernels: 8.25 us -> 3.37 us  [shards(): pl.pallas_call(emit_kernel, out_shape=[jax.ShapeDtypeStruct(a.shape, a.dt...]
where the time goes in v2:
time: 76.4 us; the launch traced here: 75.5 us
  Pallas kernels  74.9 us (98%)
    pallas_call x1, Pallas kernels, shards(): pl.pallas_call(functools.partial(layer_kernel, 1.0 / math.sqrt(RB * BLK *...  71.5 us
    pallas_call x1, Pallas kernels, shards(): pl.pallas_call(emit_kernel, out_shape=[jax.ShapeDtypeStruct(a.shape, a.dt...  3.37 us

profile of v2, /device:TPU:1, one launch (start us, length us, event | category | flops | bytes accessed | tf_op | source)
XLA Modules:
  0.0 75.5 jit_solution(2358540629306408337)
XLA Ops:
  0.6 71.5 %layer.1 = (bf16[3328,256]{1,0:T(8,128)(2,1)}, f32[128,256]{1,0:T(8,128)}, f32[128,256]{1,0:T(8,128)}, bf16[32,13312]{1,0:T(8,128)(2,1)}) custom-call(s32[2,104]{1,0:T(2,128)} %bitcast.7, s32[2,104]{1,0:T(2,128)} %bitcast.8, s32[32,2,128]{2,1,0:T(2,128)} %bitcast.5, s32[32,128]{1,0:T(8,128)} %bitcast.6, bf16[128,256]{1,0:T(8,128)(2,1)} %ws_ref.1, ...), custom_call_target="tpu_custom_call" | custom-call | flops 1800000000 | bytes 14000000 | tf_op jit(solution)/shard_map/layer/pallas_call | solution.py:698
  72.2 3.4 %emit.1 = (bf16[3328,256]{1,0:T(8,128)(2,1)}, f32[128,256]{1,0:T(8,128)}, f32[128,256]{1,0:T(8,128)}, bf16[32,13312]{1,0:T(8,128)(2,1)}) custom-call(bf16[3328,256]{1,0:T(8,128)(2,1)} %get-tuple-element.8.refs_0_, f32[128,256]{1,0:T(8,128)} %get-tuple-element.9.refs_1_, f32[128,256]{1,0:T(8,128)} %get-tuple-element.10.refs_2_, ...), custom_call_target="tpu_custom_call" | custom-call | tf_op jit(solution)/shard_map/emit/pallas_call | solution.py:715

commit v3 on v2

--- a/solution.py
+++ b/solution.py
@@ -28,6 +28,7 @@
 HALO_A = N_DOM * JB
 PARTS = ((0, 8), (8, 8), (16, 10))
 CHUNK = 2 * BLK
+EMIT_PARTS = 4
 OFFSET = (0, 1, 7, 2, 6, 3, 5, 4)
 GROUPS = ((0, 1), (1, 2), (3, 2), (5, 3))
 
@@ -88,16 +89,20 @@
     norm_factor,
     cols,
     cols_ref,
-    lists,
-    counts,
-    ws_ref,
-    wn_ref,
+    lists_hbm,
+    counts_hbm,
+    ws_hbm,
+    wn_hbm,
     x_hbm,
     adj_hbm,
     cot_hbm,
     out_hbm,
-    gs_ref,
-    gn_ref,
+    gs_hbm,
+    gn_hbm,
+    gf_hbm,
+    lists,
+    counts,
+    weights,
     gf_ref,
     x_ref,
     adj,
@@ -124,12 +129,12 @@
     q_x,
     s_z,
     w_all,
+    w_cr,
+    w_h,
     w_x,
     w_xr,
     w_zr,
     w_yr,
-    w_c,
-    w_cr,
     w_g,
     w_out,
     cols_v,
@@ -198,6 +203,16 @@
         load_own.append(cp)
     load_x = pltpu.make_async_copy(x_hbm, x_ref, loc.at[15])
     load_x.start()
+    small = []
+    for i, (src, dst) in enumerate((
+        (lists_hbm, lists),
+        (counts_hbm, counts),
+        (ws_hbm, weights.at[pl.ds(0, F), :]),
+        (wn_hbm, weights.at[pl.ds(F, F), :]),
+    )):
+        cp = pltpu.make_async_copy(src, dst, loc.at[31 + i])
+        cp.start()
+        small.append(cp)
     load_adj = pltpu.make_async_copy(adj_hbm, adj, loc.at[0])
     load_cot = pltpu.make_async_copy(cot_hbm, cot, loc.at[1])
 
@@ -279,6 +294,8 @@
         cp.start()
         h2z.append(cp)
 
+    for cp in small:
+        cp.wait()
     make_plan(d, z, cols_ref, lists, counts, cols_v, tab)
     load_plan = pltpu.make_async_copy(tab, plan, loc.at[10])
     load_plan.start()
@@ -351,7 +368,6 @@
     own_x.wait()
     for cp in xcp:
         cp.wait()
-    weights = jnp.concatenate([ws_ref[...], wn_ref[...]], axis=0)
     gcp = []
     own_g = []
     out_copies = []
@@ -363,12 +379,12 @@
         def products(i, carry, first=first):
             at = pl.ds(pl.multiple_of(first * BLK + i * CHUNK, CHUNK), CHUNK)
             panel = jnp.concatenate([xp[:, at], ap[:, at]], axis=0)
-            pre = jnp.dot(panel.T, weights, preferred_element_type=F32)
+            pre = jnp.dot(panel.T, weights[...], preferred_element_type=F32)
             sig = 1.0 / (1.0 + jnp.exp(-pre))
             out[at, :] = (pre * sig).astype(BF16)
             g = (cot[at, :].astype(F32) * sig * (1.0 + pre * (1.0 - sig))).astype(BF16)
             gp[at, :] = g
-            back = nt(weights, g).astype(BF16)
+            back = nt(weights[...], g).astype(BF16)
             bpx[:, at] = back[:F]
             bpa[:, at] = back[F:]
             return carry
@@ -394,37 +410,17 @@
         cp = pltpu.make_async_copy(out.at[here, :], out_hbm.at[here, :], loc.at[22 + n])
         cp.start()
         out_copies.append(cp)
-    dcp = []
-    for k in ys:
-        cp = remote(
-            bpx.at[pl.ds(pl.multiple_of(at_y(k) * FL, FL), FL), :],
-            dx.at[:, own_cols],
-            sd.at[k - 1],
-            rd.at[k - 1],
-            **to_y(k),
-        )
-        cp.start()
-        dcp.append(cp)
-    own_d = pltpu.make_async_copy(bpx.at[own_feats, :], dx.at[:, own_cols], loc.at[9])
-    own_d.start()
-
-    def add_core(base, first, n):
-        def body(b, carry):
-            hg[base + b] = (hg[base + b].astype(F32) + r_core[first + b].astype(F32)).astype(BF16)
-            return carry
-
-        lax.fori_loop(0, n, body, 0, unroll=8)
-
-    w_all[0:F, :] = jnp.dot(xp[...], gp[...], preferred_element_type=F32)
-    w_all[F:, :] = jnp.dot(ap[...], gp[...], preferred_element_type=F32)
     step_x = 2 * F // NX
     step_z = step_x // NZ
-    wcp = []
-    for k in xs:
-        src = w_all.at[pl.ds(pl.multiple_of(at_x(k) * step_x, step_x), step_x), :]
-        cp = remote(src, w_xr.at[k - 1], sw.at[k - 1], rw.at[k - 1], **to_x(k))
-        cp.start()
-        wcp.append(cp)
+    half_h = H // NC
+    for i, panel in enumerate((xp, ap)):
+        grad = jnp.dot(panel[...], gp[...], preferred_element_type=F32)
+        for core in range(NC):
+            w_all[core, i * F : (i + 1) * F, :] = grad[:, core * half_h : (core + 1) * half_h]
+    mine_x = pl.ds(pl.multiple_of(x * step_x, step_x), step_x)
+    mine_z = pl.ds(pl.multiple_of(z * step_z, step_z), step_z)
+    w_core = remote(w_all.at[oc], w_cr, sw.at[0], rw.at[0], **to_core)
+    w_core.start()
 
     def terms_of(q, first, count):
         def body(i, carry):
@@ -442,14 +438,12 @@
         cp.wait()
     terms_of(f, 0, RQ)
 
-    for cp in wcp:
-        cp.wait()
-    mine = pl.ds(pl.multiple_of(x * step_x, step_x), step_x)
-    w_x[...] = w_all[mine, :] + w_xr[0] + w_xr[1] + w_xr[2]
+    w_core.wait()
+    w_h[...] = w_all[c] + w_cr[...]
     wcp = []
-    for k in zs:
-        src = w_x.at[pl.ds(pl.multiple_of(at_z(k) * step_z, step_z), step_z), :]
-        cp = remote(src, w_zr.at[k - 1], sw.at[2 + k], rw.at[2 + k], **to_z(k))
+    for k in xs:
+        src = w_h.at[pl.ds(pl.multiple_of(at_x(k) * step_x, step_x), step_x), :]
+        cp = remote(src, w_xr.at[k - 1], sw.at[k], rw.at[k], **to_x(k))
         cp.start()
         wcp.append(cp)
 
@@ -457,6 +451,16 @@
         for k in ys:
             gcp[n * 3 + k - 1].wait()
             terms_of(at_y(NY - k), first, count)
+        if n == 1:
+            for cp in wcp:
+                cp.wait()
+            w_x[...] = w_h[mine_x, :] + w_xr[0] + w_xr[1] + w_xr[2]
+            wcp = []
+            for k in zs:
+                src = w_x.at[pl.ds(pl.multiple_of(at_z(k) * step_z, step_z), step_z), :]
+                cp = remote(src, w_zr.at[k - 1], sw.at[3 + k], rw.at[3 + k], **to_z(k))
+                cp.start()
+                wcp.append(cp)
 
     def chain(r, carry):
         terms0[r] = terms0[r] + terms0[plan[1, r]]
@@ -501,15 +505,36 @@
 
     for cp in wcp:
         cp.wait()
-    acc = w_x[pl.ds(pl.multiple_of(z * step_z, step_z), step_z), :]
+    acc = w_x[mine_z, :]
     for k in zs:
         acc = acc + w_zr[k - 1]
     w_yr[f] = acc
     wcp = []
     for k in ys:
-        cp = remote(w_yr.at[f], w_yr.at[f], sw.at[9 + k], rw.at[9 + k], **to_y(k))
+        cp = remote(w_yr.at[f], w_yr.at[f], sw.at[10 + k], rw.at[10 + k], **to_y(k))
         cp.start()
         wcp.append(cp)
+
+    dcp = []
+    for k in ys:
+        cp = remote(
+            bpx.at[pl.ds(pl.multiple_of(at_y(k) * FL, FL), FL), :],
+            dx.at[:, own_cols],
+            sd.at[k - 1],
+            rd.at[k - 1],
+            **to_y(k),
+        )
+        cp.start()
+        dcp.append(cp)
+    own_d = pltpu.make_async_copy(bpx.at[own_feats, :], dx.at[:, own_cols], loc.at[9])
+    own_d.start()
+
+    def add_core(base, first, n):
+        def body(b, carry):
+            hg[base + b] = (hg[base + b].astype(F32) + r_core[first + b].astype(F32)).astype(BF16)
+            return carry
+
+        lax.fori_loop(0, n, body, 0, unroll=8)
 
     for i, k in enumerate((1, 3, 2)):
         core_copies[i].wait()
@@ -538,21 +563,15 @@
         c1z.append(cp)
     for cp in wcp:
         cp.wait()
-    w_c[...] = ((w_yr[0] + w_yr[1]) + w_yr[2]) + w_yr[3]
-    w_core = remote(w_c, w_cr, sw.at[13], rw.at[13], **to_core)
-    w_core.start()
+    w_g[mine_z, :] = (((w_yr[0] + w_yr[1]) + w_yr[2]) + w_yr[3]) * norm_factor
+    wcp = []
+    for k in zs:
+        cp = remote(w_g.at[mine_z, :], w_g.at[mine_z, :], sw.at[13 + k], rw.at[13 + k], **to_z(k))
+        cp.start()
+        wcp.append(cp)
 
     core_copies[3].wait()
     add_core(c * half_b + x * row_b, x * row_b, row_b)
-    w_core.wait()
-    w_g[pl.ds(pl.multiple_of(z * step_z, step_z), step_z), :] = (w_c[...] + w_cr[...]) * norm_factor
-    wcp = []
-    for k in zs:
-        src = w_g.at[pl.ds(pl.multiple_of(z * step_z, step_z), step_z), :]
-        cp = remote(src, src, sw.at[13 + k], rw.at[13 + k], **to_z(k))
-        cp.start()
-        wcp.append(cp)
-
     c2z = []
     for g in (3, 2, 1, 0):
         for cp in c1x[g]:
@@ -580,15 +599,21 @@
                 cp = remote(s_z.at[at_x(k)], q_x.at[k - 1], sr.at[23 + k], rr.at[23 + k], **to_x(k))
                 cp.start()
                 c2x.append(cp)
-        if g == 1:
+        if g == 3:
             for cp in wcp:
                 cp.wait()
-            w_out[mine, :] = w_g[...]
+            w_out[c, mine_x, :] = w_g[...]
             wcp = []
             for k in xs:
-                cp = remote(w_g, w_out.at[mine, :], sw.at[20 + k], rw.at[20 + k], **to_x(k))
+                cp = remote(w_g, w_out.at[c, mine_x, :], sw.at[20 + k], rw.at[20 + k], **to_x(k))
                 cp.start()
                 wcp.append(cp)
+
+        if g == 0:
+            for cp in wcp:
+                cp.wait()
+            w_core = remote(w_out.at[c], w_out.at[c], sw.at[24], rw.at[24], **to_core)
+            w_core.start()
 
     own_d.wait()
     for cp in dcp:
@@ -600,6 +625,9 @@
         return carry
 
     lax.fori_loop(BND, RB, finish, 0, unroll=10)
+    tail = pl.ds(BND * BLK, (RB - BND) * BLK)
+    put_tail = pltpu.make_async_copy(gf_ref.at[:, tail], gf_hbm.at[:, tail], loc.at[25])
+    put_tail.start()
     for cp in c2x + c2z:
         cp.wait()
     for j in range(BND):
@@ -615,20 +643,42 @@
                 acc = acc + q_x[k - 1].astype(F32)
         gf_ref[:, at] = acc.astype(BF16)
 
-    for cp in wcp:
-        cp.wait()
-    gs_ref[...] = w_out[:F, :]
-    gn_ref[...] = w_out[F:, :]
-    for cp in out_copies:
+    head = pl.ds(0, BND * BLK)
+    put_head = pltpu.make_async_copy(gf_ref.at[:, head], gf_hbm.at[:, head], loc.at[26])
+    put_head.start()
+
+    w_core.wait()
+    puts = []
+    for core in range(NC):
+        for i, dst in enumerate((gs_hbm, gn_hbm)):
+            cp = pltpu.make_async_copy(
+                w_out.at[core, pl.ds(i * F, F), :],
+                dst.at[:, pl.ds(core * half_h, half_h)],
+                loc.at[27 + 2 * core + i],
+            )
+            cp.start()
+            puts.append(cp)
+    for cp in out_copies + puts + [put_tail, put_head]:
         cp.wait()
 
 
 def emit_kernel(*refs):
-    copies = [pltpu.make_async_copy(refs[i], refs[4 + i], refs[8].at[i]) for i in range(4)]
-    for cp in copies:
-        cp.start()
-    for cp in copies:
-        cp.wait()
+    sems = refs[12]
+    pieces = []
+    for src, dst, held in zip(refs[:4], refs[4:8], refs[8:12]):
+        parts = EMIT_PARTS if src.shape[0] * src.shape[1] > 2 * F * H else 1
+        rows = src.shape[0] // parts
+        for p in range(parts):
+            at = pl.ds(p * rows, rows)
+            n = 2 * len(pieces)
+            into = pltpu.make_async_copy(src.at[at, :], held.at[at, :], sems.at[n])
+            into.start()
+            pieces.append((into, pltpu.make_async_copy(held.at[at, :], dst.at[at, :], sems.at[n + 1])))
+    for into, out in pieces:
+        into.wait()
+        out.start()
+    for _, out in pieces:
+        out.wait()
 
 
 def shards(node_feats, adj_cols, adj_vals, send_list, send_count, w_self, w_neigh, cotangent):
@@ -640,9 +690,14 @@
     hbm = pl.BlockSpec(memory_space=pl.ANY)
     vm = pltpu.VMEM
     dma = pltpu.SemaphoreType.DMA
+    half_h = H // NC
     step_x = 2 * F // NX
     step_z = step_x // NZ
     scratch = [
+        vm((NX * NZ, CAP, NC * N_DOM), jnp.int32),
+        vm((NX * NZ, NC * N_DOM), jnp.int32),
+        vm((2 * F, H), BF16),
+        vm((FL, RB * BLK), BF16),
         vm((FL, RB * BLK), BF16),
         vm((RB, 2, BLK, BLK), BF16),
         vm((ROWS, H), BF16),
@@ -667,19 +722,19 @@
         vm((NZ - 1, JB, FL, BLK), BF16),
         vm((NX - 1, FL, BLK), BF16),
         vm((NX, FL, BLK), BF16),
-        vm((2 * F, H), F32),
-        vm((step_x, H), F32),
-        vm((NX - 1, step_x, H), F32),
-        vm((NZ - 1, step_z, H), F32),
-        vm((NY, step_z, H), F32),
-        vm((step_z, H), F32),
-        vm((step_z, H), F32),
-        vm((step_x, H), F32),
-        vm((2 * F, H), F32),
+        vm((NC, 2 * F, half_h), F32),
+        vm((2 * F, half_h), F32),
+        vm((2 * F, half_h), F32),
+        vm((step_x, half_h), F32),
+        vm((NX - 1, step_x, half_h), F32),
+        vm((NZ - 1, step_z, half_h), F32),
+        vm((NY, step_z, half_h), F32),
+        vm((step_x, half_h), F32),
+        vm((NC, 2 * F, half_h), F32),
         vm((8, BLK), jnp.int32),
         vm((8, BLK), jnp.int32),
         pltpu.SMEM((8, BLK), jnp.int32),
-        dma((25,)),
+        dma((35,)),
         dma((3,)),
         dma((3,)),
         dma((9,)),
@@ -692,8 +747,8 @@
         dma((42,)),
         dma((34,)),
         dma((34,)),
-        dma((24,)),
-        dma((24,)),
+        dma((25,)),
+        dma((25,)),
     ]
     results = pl.pallas_call(
         functools.partial(layer_kernel, 1.0 / math.sqrt(RB * BLK * N_DOM)),
@@ -703,8 +758,8 @@
             jax.ShapeDtypeStruct((F, H), F32),
             jax.ShapeDtypeStruct((FL, RB * BLK), BF16),
         ),
-        in_specs=[smem] + [vmem] * 5 + [hbm] * 3,
-        out_specs=(hbm, vmem, vmem, vmem),
+        in_specs=[smem, vmem] + [hbm] * 7,
+        out_specs=(hbm, hbm, hbm, hbm),
         scratch_shapes=scratch,
         compiler_params=pltpu.CompilerParams(
             collective_id=0, has_side_effects=True, vmem_limit_bytes=56 * 1024 * 1024
@@ -715,9 +770,10 @@
     return pl.pallas_call(
         emit_kernel,
         out_shape=[jax.ShapeDtypeStruct(a.shape, a.dtype) for a in results],
-        in_specs=[vmem] * 4,
+        in_specs=[hbm] * 4,
         out_specs=[hbm] * 4,
-        scratch_shapes=[dma((4,))],
+        scratch_shapes=[vm(a.shape, a.dtype) for a in results] + [dma((4 * EMIT_PARTS + 4,))],
+        compiler_params=pltpu.CompilerParams(vmem_limit_bytes=56 * 1024 * 1024),
         name="emit",
     )(*results)
 

time: 76.4 us -> 74.2 us (0.971)
  Pallas kernels: 74.9 us -> 73.4 us
    pallas_call x1, Pallas kernels: 71.5 us -> 70.7 us  [shards(): pl.pallas_call(functools.partial(layer_kernel, 1.0 / math.sqrt(RB * BLK *...]
where the time goes in v3:
time: 74.2 us; the launch traced here: 74.1 us
  Pallas kernels  73.4 us (99%)
    pallas_call x1, Pallas kernels, shards(): pl.pallas_call(functools.partial(layer_kernel, 1.0 / math.sqrt(RB * BLK *...  70.7 us
    pallas_call x1, Pallas kernels, shards(): pl.pallas_call(emit_kernel, out_shape=[jax.ShapeDtypeStruct(a.shape, a.dt...  2.72 us

profile of v3, /device:TPU:1, one launch (start us, length us, event | category | flops | bytes accessed | tf_op | source)
XLA Modules:
  0.0 74.1 jit_solution(14853001273352334365)
XLA Ops:
  0.6 70.7 %layer.1 = (bf16[3328,256]{1,0:T(8,128)(2,1)}, f32[128,256]{1,0:T(8,128)}, f32[128,256]{1,0:T(8,128)}, bf16[32,13312]{1,0:T(8,128)(2,1)}) custom-call(s32[2,104]{1,0:T(2,128)} %bitcast.7, s32[2,104]{1,0:T(2,128)} %bitcast.8, s32[32,2,128]{2,1,0:T(2,128)} %bitcast.5, s32[32,128]{1,0:T(8,128)} %bitcast.6, bf16[128,256]{1,0:T(8,128)(2,1)} %ws_hbm.1, ...), custom_call_target="tpu_custom_call" | custom-call | flops 1800000000 | bytes 14000000 | tf_op jit(solution)/shard_map/layer/pallas_call | solution.py:753
  71.3 2.7 %emit.1 = (bf16[3328,256]{1,0:T(8,128)(2,1)}, f32[128,256]{1,0:T(8,128)}, f32[128,256]{1,0:T(8,128)}, bf16[32,13312]{1,0:T(8,128)(2,1)}) custom-call(bf16[3328,256]{1,0:T(8,128)(2,1)} %get-tuple-element.8.refs_0_, f32[128,256]{1,0:T(8,128)} %get-tuple-element.9.refs_1_, f32[128,256]{1,0:T(8,128)} %get-tuple-element.10.refs_2_, ...), custom_call_target="tpu_custom_call" | custom-call | tf_op jit(solution)/shard_map/emit/pallas_call | solution.py:770

commit v4 on v3

--- a/solution.py
+++ b/solution.py
@@ -628,6 +628,17 @@
     tail = pl.ds(BND * BLK, (RB - BND) * BLK)
     put_tail = pltpu.make_async_copy(gf_ref.at[:, tail], gf_hbm.at[:, tail], loc.at[25])
     put_tail.start()
+    w_core.wait()
+    puts = []
+    for core in range(NC):
+        for i, dst in enumerate((gs_hbm, gn_hbm)):
+            cp = pltpu.make_async_copy(
+                w_out.at[core, pl.ds(i * F, F), :],
+                dst.at[:, pl.ds(core * half_h, half_h)],
+                loc.at[27 + 2 * core + i],
+            )
+            cp.start()
+            puts.append(cp)
     for cp in c2x + c2z:
         cp.wait()
     for j in range(BND):
@@ -647,17 +658,6 @@
     put_head = pltpu.make_async_copy(gf_ref.at[:, head], gf_hbm.at[:, head], loc.at[26])
     put_head.start()
 
-    w_core.wait()
-    puts = []
-    for core in range(NC):
-        for i, dst in enumerate((gs_hbm, gn_hbm)):
-            cp = pltpu.make_async_copy(
-                w_out.at[core, pl.ds(i * F, F), :],
-                dst.at[:, pl.ds(core * half_h, half_h)],
-                loc.at[27 + 2 * core + i],
-            )
-            cp.start()
-            puts.append(cp)
     for cp in out_copies + puts + [put_tail, put_head]:
         cp.wait()
 
@@ -666,8 +666,8 @@
     sems = refs[12]
     pieces = []
     for src, dst, held in zip(refs[:4], refs[4:8], refs[8:12]):
-        parts = EMIT_PARTS if src.shape[0] * src.shape[1] > 2 * F * H else 1
-        rows = src.shape[0] // parts
+        rows = min(src.shape[0], max(16, src.shape[0] // EMIT_PARTS // 16 * 16)) if src.dtype == BF16 else src.shape[0]
+        parts = src.shape[0] // rows
         for p in range(parts):
             at = pl.ds(p * rows, rows)
             n = 2 * len(pieces)

time: 74.2 us -> 74.1 us (level)
  no operation moved by 1% of the time
where the time goes in v4:
time: 74.1 us; the launch traced here: 74 us
  Pallas kernels  73.3 us (99%)
    pallas_call x1, Pallas kernels, shards(): pl.pallas_call(functools.partial(layer_kernel, 1.0 / math.sqrt(RB * BLK *...  70.6 us
    pallas_call x1, Pallas kernels, shards(): pl.pallas_call(emit_kernel, out_shape=[jax.ShapeDtypeStruct(a.shape, a.dt...  2.73 us

profile of v4, /device:TPU:1, one launch (start us, length us, event | category | flops | bytes accessed | tf_op | source)
XLA Modules:
  0.0 74.0 jit_solution(11166277106497617731)
XLA Ops:
  0.6 70.6 %layer.1 = (bf16[3328,256]{1,0:T(8,128)(2,1)}, f32[128,256]{1,0:T(8,128)}, f32[128,256]{1,0:T(8,128)}, bf16[32,13312]{1,0:T(8,128)(2,1)}) custom-call(s32[2,104]{1,0:T(2,128)} %bitcast.7, s32[2,104]{1,0:T(2,128)} %bitcast.8, s32[32,2,128]{2,1,0:T(2,128)} %bitcast.5, s32[32,128]{1,0:T(8,128)} %bitcast.6, bf16[128,256]{1,0:T(8,128)(2,1)} %ws_hbm.1, ...), custom_call_target="tpu_custom_call" | custom-call | flops 1800000000 | bytes 14000000 | tf_op jit(solution)/shard_map/layer/pallas_call | solution.py:753
  71.2 2.7 %emit.1 = (bf16[3328,256]{1,0:T(8,128)(2,1)}, f32[128,256]{1,0:T(8,128)}, f32[128,256]{1,0:T(8,128)}, bf16[32,13312]{1,0:T(8,128)(2,1)}) custom-call(bf16[3328,256]{1,0:T(8,128)(2,1)} %get-tuple-element.8.refs_0_, f32[128,256]{1,0:T(8,128)} %get-tuple-element.9.refs_1_, f32[128,256]{1,0:T(8,128)} %get-tuple-element.10.refs_2_, ...), custom_call_target="tpu_custom_call" | custom-call | tf_op jit(solution)/shard_map/emit/pallas_call | solution.py:770
